TPU v7x, 512 devices: a whole 4x4x16 slice. The times are simulated.
512 devices in a mesh: snap: 16 (over x, y), vert: 32 (over z, core).
Axes of the slice: x: 4, y: 4, z: 16, core: 2. Of those that a mesh axis runs over, the one named last changes fastest.
Arguments:
- features: bfloat16 [16, 16384, 256], P('snap', 'vert'), may hold values from -6 to 6
- tile_src: int32 [16, 1024], P('snap', 'vert'), may hold values from 0 to 127, as said below
- tile_dst: int32 [16, 1024], P('snap', 'vert'), may hold values from 0 to 127, as said below
- tile_count: int32 [16, 32], P('snap', 'vert'), may hold values from 4 to 32, as said below
- tile_vals: bfloat16 [16, 1024, 128, 128], P('snap', 'vert'), may hold values from -0.25 to 0.25
- norm_gain: float32 [256], replicated, may hold values from 0.25 to 1.75
- mix_weight: bfloat16 [256, 512], replicated, may hold values from -0.375 to 0.375
- decay_rate: float32 [16, 256], replicated, may hold values from 0 to 9, as said below
- mlp_gain: float32 [256], replicated, may hold values from 0.25 to 1.75
- up_weight: bfloat16 [256, 1024], replicated, may hold values from -0.375 to 0.375
- down_weight: bfloat16 [1024, 256], replicated, may hold values from -0.1875 to 0.1875
- link_weight: bfloat16 [256, 256], replicated, may hold values from -0.375 to 0.375
- pair_left: int32 [16, 1024], P('snap', 'vert'), may hold values from 0 to 127, as said below
- pair_right: int32 [16, 1024], P('snap', 'vert'), may hold values from 0 to 127, as said below
Outputs:
- embeddings: bfloat16 [16, 16384, 256], P('snap', 'vert')
- scores: bfloat16 [16, 1024, 128, 128], P('snap', 'vert')
Inputs may be any that keep to these rules, and one draw needn't show every extreme that they name: `tile_src`: a slot of vertex part p names a source block from p * 4 - 4 to p * 4 + 2 * 4 - 1. `tile_dst`: a slot of vertex part p names a destination block of that part, p * 4 to p * 4 + 3. `tile_count`: in every snapshot some vertex part has all 32 slots live. `decay_rate`: decay rates are positive. `pair_left`: a pair of vertex part p has its first block in that part, p * 4 to p * 4 + 3. `pair_right`: a pair of vertex part p has its second block from p * 4 - 4 to p * 4 + 2 * 4 - 1.
All inputs are finite; a program needn't handle non-finite values.
Results may differ from a plain program's by a relative error of at most 0.0091.
Values may be sent and summed in bfloat16 or wider, within the bound.
No kernel may reach another device: no remote copies, remote signals or barrier semaphores. Data moves between devices by JAX's collectives and lax.ppermute only.
A program may use at most 64 MiB of HBM per device.

v0:
```python
import jax
import jax.numpy as jnp
from jax import lax
from jax.sharding import PartitionSpec as P

epsilon = 1e-06


def with_halo(cells, sides, width):
    for axis, dim in sides:
        count = lax.axis_size(axis)
        ends = count - 1
        head = lax.slice_in_dim(cells, 0, width, axis=dim)
        tail = lax.slice_in_dim(cells, cells.shape[dim] - width, cells.shape[dim], axis=dim)
        cells = jnp.concatenate(
            [
                lax.ppermute(tail, axis, [(i, (i + 1) % count) for i in range(ends)]),
                cells,
                lax.ppermute(head, axis, [((i + 1) % count, i) for i in range(ends)]),
            ],
            axis=dim,
        )
    return cells


def root_norm(values, gain_vector):
    return (
        values
        * lax.rsqrt(jnp.mean(values * values, axis=-1, keepdims=True) + epsilon)
        * gain_vector
    )


def pick_blocks(blocks, indices):
    return jax.vmap(lambda source_table, chosen: jnp.take(source_table, chosen, axis=0))(
        blocks, indices
    )


def tile_terms(blocks, src_index, dst_index, tile_part, alive_slots, per_part):
    picked = pick_blocks(blocks, src_index)
    product = jnp.einsum("sgij,sgjf->sgif", tile_part, picked, preferred_element_type=jnp.float32)
    targets = jnp.arange(per_part, dtype=jnp.int32)[None, None, :]
    selector = ((dst_index[:, :, None] == targets) & alive_slots[:, :, None]).astype(jnp.float32)
    return jnp.einsum("sgb,sgif->sbif", selector, product, precision=lax.Precision.HIGHEST)


def gate_drive(normed, step_rates, mix_weight):
    projected = jnp.einsum("tnf,fg->tng", normed, mix_weight, preferred_element_type=jnp.float32)
    feature_width = normed.shape[-1]
    decays = jnp.exp(-step_rates[:, None, :] * jax.nn.sigmoid(projected[..., :feature_width]))
    return (decays, (1.0 - decays) * projected[..., feature_width:])


def advance(previous, inputs):
    updated = inputs[0] * previous + inputs[1]
    return (updated, updated)


def run_states(decays, drives, start_state):
    final_state, states = lax.scan(advance, start_state, (decays, drives))
    return states


def feed_forward(states, mlp_gain, up_weight, down_weight):
    state_normed = root_norm(states, mlp_gain).astype(jnp.bfloat16)
    hidden = jax.nn.silu(
        jnp.einsum("tnf,fh->tnh", state_normed, up_weight, preferred_element_type=jnp.float32)
    ).astype(jnp.bfloat16)
    return (
        states + jnp.einsum("tnh,hf->tnf", hidden, down_weight, preferred_element_type=jnp.float32)
    ).astype(jnp.bfloat16)


def body(
    features,
    tile_src,
    tile_dst,
    tile_count,
    tile_vals,
    norm_gain,
    mix_weight,
    decay_rate,
    mlp_gain,
    up_weight,
    down_weight,
    link_weight,
    pair_left,
    pair_right,
):
    snaps_here, vertices_here, feature_width = features.shape
    tile_rows = tile_vals.shape[-1]
    slot_count = tile_vals.shape[1]
    per_part = vertices_here // tile_rows
    part_index = lax.axis_index("vert")
    first_block = (part_index - 1) * per_part
    own_first = part_index * per_part
    extended = with_halo(features, (("vert", 1),), vertices_here)
    blocks = extended.reshape(snaps_here, 3 * per_part, tile_rows, feature_width)
    local_src = tile_src - first_block
    local_dst = tile_dst - own_first
    slot_ids = jnp.arange(slot_count, dtype=jnp.int32)[None, :]
    aggregate = tile_terms(blocks, local_src, local_dst, tile_vals, slot_ids < tile_count, per_part)
    combined = aggregate.reshape(snaps_here, vertices_here, feature_width) + features.astype(
        jnp.float32
    )
    normed = root_norm(combined, norm_gain).astype(jnp.bfloat16)
    by_vertex = lax.all_to_all(normed, "snap", split_axis=1, concat_axis=0, tiled=True)
    decays, drives = gate_drive(by_vertex, decay_rate, mix_weight)
    states = run_states(decays, drives, jnp.zeros(decays.shape[1:], jnp.float32))
    vertex_out = feed_forward(states, mlp_gain, up_weight, down_weight)
    embeddings = lax.all_to_all(vertex_out, "snap", split_axis=0, concat_axis=1, tiled=True)
    extended_out = with_halo(embeddings, (("vert", 1),), vertices_here)
    left_side = jnp.einsum(
        "svf,fg->svg", embeddings, link_weight, preferred_element_type=jnp.float32
    ).astype(jnp.bfloat16)
    left_blocks = pick_blocks(
        left_side.reshape(snaps_here, per_part, tile_rows, feature_width), pair_left - own_first
    )
    right_blocks = pick_blocks(
        extended_out.reshape(snaps_here, 3 * per_part, tile_rows, feature_width),
        pair_right - first_block,
    )
    scores = jnp.einsum(
        "spif,spjf->spij", left_blocks, right_blocks, preferred_element_type=jnp.float32
    ) * feature_width ** (-0.5)
    return (embeddings, scores.astype(jnp.bfloat16))


def solution(mesh):
    return jax.shard_map(
        body,
        mesh=mesh,
        in_specs=(
            P("snap", "vert", None),
            P("snap", "vert"),
            P("snap", "vert"),
            P("snap", "vert"),
            P("snap", "vert", None, None),
            P(),
            P(),
            P(),
            P(),
            P(),
            P(),
            P(),
            P("snap", "vert"),
            P("snap", "vert"),
        ),
        out_specs=(P("snap", "vert", None), P("snap", "vert", None, None)),
        check_vma=False,
    )
```

profile of v0, /device:TPU:97, one launch (start us, length us, event | category | flops | bytes accessed | tf_op | source)
XLA Modules:
  0.0 86.9 jit_solution(15219343378757450271)
XLA Ops:
  0.6 0.0 copy-start
  0.6 5.5 %collective-permute-start = (bf16[1,512,256]{2,1,0:T(8,128)(2,1)}, bf16[1,512,256]{2,1,0:T(8,128)(2,1)S(1)}, u32[]{:S(2)}, u32[]{:S(2)}) collective-permute-start(bf16[1,512,256]{2,1,0:T(8,128)(2,1)} %param.18), channel_id=1, source_target_pairs={{0,1},{1,2},{2,3},{3,4},{4,5},{5,6},{6,7},{7,8},{8,9},{9,10},{10,1... | collective-permute-start | bytes 786440 | tf_op jit(solution)/shard_map/ppermute | solution.py:17
  6.1 1.9 %collective-permute-start.1 = (bf16[1,512,256]{2,1,0:T(8,128)(2,1)}, bf16[1,512,256]{2,1,0:T(8,128)(2,1)S(1)}, u32[]{:S(2)}, u32[]{:S(2)}) collective-permute-start(bf16[1,512,256]{2,1,0:T(8,128)(2,1)} %param.18), channel_id=1, source_target_pairs={{1,0},{2,1},{3,2},{4,3},{5,4},{6,5},{7,6},{8,7},{9,8},{10,9},{11,1... | collective-permute-start | bytes 786440 | tf_op jit(solution)/shard_map/ppermute | solution.py:19
  8.0 0.7 and_bitcast_fusion.1
  9.4 0.7 subtract_bitcast_fusion
  10.0 0.7 neg.11
  10.8 0.0 collective-permute-done
  10.8 4.4 %collective-permute-done.1 = bf16[1,512,256]{2,1,0:T(8,128)(2,1)S(1)} collective-permute-done((bf16[1,512,256]{2,1,0:T(8,128)(2,1)}, bf16[1,512,256]{2,1,0:T(8,128)(2,1)S(1)}, u32[]{:S(2)}, u32[]{:S(2)}) %collective-permute-start.1) | collective-permute-done | bytes 262176 | tf_op jit(solution)/shard_map/ppermute | solution.py:19
  15.2 1.0 %pad_maximum_fusion = bf16[1,1536,256]{2,1,0:T(8,128)(2,1)S(1)} fusion(bf16[1,512,256]{2,1,0:T(8,128)(2,1)S(1)} %collective-permute-done.1, bf16[1,512,256]{2,1,0:T(8,128)(2,1)} %param.18, bf16[1,512,256]{2,1,0:T(8,128)(2,1)S(1)} %collective-permute-done), kind=kLoop, calls=%fused_computation.27 | loop fusion | flops 2359296 | bytes 1572864 | tf_op jit(solution)/shard_map/concatenate | solution.py:15
  16.2 2.0 %gather_fusion.1 = bf16[32,128,256]{2,1,0:T(8,128)(2,1)} fusion(bf16[1,12,128,256]{3,2,1,0:T(8,128)(2,1)S(1)} %bitcast.104, s32[32]{0:T(128)S(1)} %or_bitcast_fusion.1), kind=kCustom, calls=%fused_computation.clone | custom fusion | bytes 4194560 | tf_op jit(solution)/shard_map/vmap(jit(_take))/gather | solution.py:35
  18.2 0.0 copy-done
  18.2 4.4 %convolution_bitcast_fusion = f32[32,128,256]{1,2,0:T(8,128)} fusion(bf16[32,128,256]{2,1,0:T(8,128)(2,1)} %gather_fusion.1, pred[32]{0:T(512)(128)(4,1)S(1)} %get-tuple-element.67, bf16[1,32,128,128]{3,2,1,0:T(8,128)(2,1)S(1)} %copy-done), kind=kOutput, calls=%fused_computation.6 | convolution fusion | flops 269484032 | bytes 7340064 | tf_op jit(solution)/shard_map/sgij,sgjf->sgif/dot_general | solution.py:42
  22.6 5.5 %copy.21 = f32[32,128,256]{2,0,1:T(8,128)} copy(f32[32,128,256]{1,2,0:T(8,128)} %convolution_bitcast_fusion) | data formatting | bytes 8388608 | tf_op jit(solution)/shard_map/sgij,sgjf->sgif/dot_general | solution.py:42
  28.1 0.0 copy-start.1
  28.1 0.0 copy-start.4
  28.1 3.7 %fusion.38 = f32[4,128,256]{2,0,1:T(4,128)S(1)} fusion(f32[32,128,256]{2,0,1:T(8,128)} %copy.21, s32[32]{0:T(128)S(1)} %subtract_bitcast_fusion, pred[32]{0:T(512)(128)(4,1)S(1)} %iota_compare_fusion.1), kind=kOutput, calls=%fused_computation.55 | convolution fusion | flops 50331904 | bytes 4718752 | tf_op jit(solution)/shard_map/sgb,sgif->sbif/dot_general | solution.py:45
  31.8 0.1 copy.22
  31.9 0.0 copy-done.1
  31.9 0.0 copy-start.5
  31.9 0.0 copy-start.6
  31.9 0.2 multiply_reduce_fusion.1
  32.1 0.0 copy-done.4
  32.1 0.1 multiply_convert_fusion.5
  32.2 0.0 copy-start.2
  32.3 0.4 copy.27
  32.7 0.5 broadcast.170
  33.2 2.2 %reduce.1 = bf16[512,256]{1,0:T(8,128)(2,1)S(1)} reduce(bf16[512,1,256]{2,1,0:T(2,128)(2,1)S(1)} %bitcast.114, bf16[]{:T(256)} %broadcast.170), dimensions={1}, to_apply=%bitcast.97.reduce_sub_computation | reduce | bytes 524290
  35.4 0.8 reshape.205
  36.2 6.8 %all-to-all-start = ((bf16[16,2,4096]{2,1,0:T(2,128)(2,1)}), bf16[16,2,4096]{2,1,0:T(2,128)(2,1)S(1)}, u32[]{:S(2)}, u32[]{:S(2)}) async-start(bf16[16,2,4096]{2,1,0:T(2,128)(2,1)} %reshape.205), calls=%async_computation | async-start | bytes 524288 | tf_op jit(solution)/shard_map/all_to_all | solution.py:108
  42.9 0.0 copy-done.5
  42.9 0.0 copy-done.6
  43.0 7.3 %all-to-all-done = bf16[16,2,4096]{2,1,0:T(2,128)(2,1)S(1)} async-done(((bf16[16,2,4096]{2,1,0:T(2,128)(2,1)}), bf16[16,2,4096]{2,1,0:T(2,128)(2,1)S(1)}, u32[]{:S(2)}, u32[]{:S(2)}) %all-to-all-start) | async-done | bytes 262176 | tf_op jit(solution)/shard_map/all_to_all | solution.py:108
  50.3 0.3 reshape.206
  50.6 0.0 copy-done.2
  50.6 0.3 fusion.30
  50.9 0.0 copy-start.7
  50.9 0.2 slice_multiply_fusion
  51.1 0.6 while.13
  51.8 0.1 multiply_reduce_fusion
  51.9 0.0 copy-done.7
  52.0 0.0 copy-start.3
  52.0 2.8 %fusion.16 = bf16[16,32,256]{2,1,0:T(8,128)(2,1)} fusion(f32[16,32,256]{2,1,0:T(8,128)S(1)} %get-tuple-element.30, bf16[1024,256]{1,0:T(8,128)(2,1)} %param.28, bf16[256,1024]{1,0:T(8,128)(2,1)} %param.27, f32[256]{0:T(256)S(1)} %copy-done.7, f32[16,32]{1,0:T(8,128)S(1)} %add_rsqrt_fusion), kind=kOutput, calls=%fused_computation.20 | convolution fusion | flops 540147712 | bytes 1838080 | tf_op jit(solution)/shard_map/tnh,hf->tnf/dot_general | solution.py:71
  54.8 3.5 %all-to-all-start.1 = ((bf16[16,32,256]{2,1,0:T(8,128)(2,1)}), bf16[16,32,256]{2,1,0:T(8,128)(2,1)S(1)}, u32[]{:S(2)}, u32[]{:S(2)}) async-start(bf16[16,32,256]{2,1,0:T(8,128)(2,1)} %fusion.16), calls=%async_computation.1 | async-start | bytes 524288 | tf_op jit(solution)/shard_map/all_to_all | solution.py:112
  58.4 7.3 %all-to-all-done.1 = bf16[16,32,256]{2,1,0:T(8,128)(2,1)S(1)} async-done(((bf16[16,32,256]{2,1,0:T(8,128)(2,1)}), bf16[16,32,256]{2,1,0:T(8,128)(2,1)S(1)}, u32[]{:S(2)}, u32[]{:S(2)}) %all-to-all-start.1) | async-done | bytes 262176 | tf_op jit(solution)/shard_map/all_to_all | solution.py:112
  65.6 5.6 %collective-permute-start.2 = (bf16[1,512,256]{2,1,0:T(8,128)(2,1)S(1)}, bf16[1,512,256]{2,1,0:T(8,128)(2,1)S(1)}, u32[]{:S(2)}, u32[]{:S(2)}) collective-permute-start(bf16[1,512,256]{2,1,0:T(8,128)(2,1)S(1)} %bitcast.108), channel_id=1, source_target_pairs={{0,1},{1,2},{2,3},{3,4},{4,5},{5,6},{6,7},{7,8},{8,9},{9,10},{10,1... | collective-permute-start | bytes 786440 | tf_op jit(solution)/shard_map/ppermute | solution.py:17
  71.3 1.9 %collective-permute-start.3 = (bf16[1,512,256]{2,1,0:T(8,128)(2,1)S(1)}, bf16[1,512,256]{2,1,0:T(8,128)(2,1)S(1)}, u32[]{:S(2)}, u32[]{:S(2)}) collective-permute-start(bf16[1,512,256]{2,1,0:T(8,128)(2,1)S(1)} %bitcast.109), channel_id=1, source_target_pairs={{1,0},{2,1},{3,2},{4,3},{5,4},{6,5},{7,6},{8,7},{9,8},{10,9},{11,1... | collective-permute-start | bytes 786440 | tf_op jit(solution)/shard_map/ppermute | solution.py:19
  73.2 0.0 copy-done.3
  73.2 0.2 convolution_convert_fusion
  73.5 2.0 %gather_fusion = bf16[32,128,256]{2,1,0:T(8,128)(2,1)} fusion(bf16[1,4,128,256]{3,2,1,0:T(8,128)(2,1)S(1)} %bitcast.103, s32[32]{0:T(128)S(1)} %or_bitcast_fusion.2), kind=kCustom, calls=%fused_computation.2 | custom fusion | bytes 4194560 | tf_op jit(solution)/shard_map/vmap(jit(_take))/gather | solution.py:35
  75.5 0.0 collective-permute-done.2
  75.5 4.7 %collective-permute-done.3 = bf16[1,512,256]{2,1,0:T(8,128)(2,1)S(1)} collective-permute-done((bf16[1,512,256]{2,1,0:T(8,128)(2,1)S(1)}, bf16[1,512,256]{2,1,0:T(8,128)(2,1)S(1)}, u32[]{:S(2)}, u32[]{:S(2)}) %collective-permute-start.3) | collective-permute-done | bytes 262176 | tf_op jit(solution)/shard_map/ppermute | solution.py:19
  80.2 0.1 pad_maximum_fusion.1
  80.2 2.0 %gather_fusion.2 = bf16[32,128,256]{2,1,0:T(8,128)(2,1)} fusion(bf16[1,12,128,256]{3,2,1,0:T(8,128)(2,1)S(1)} %bitcast.105, s32[32]{0:T(128)S(1)} %or_bitcast_fusion), kind=kCustom, calls=%fused_computation.1.clone | custom fusion | bytes 4194560 | tf_op jit(solution)/shard_map/vmap(jit(_take))/gather | solution.py:35
  82.2 4.0 %fusion.11 = bf16[1,32,128,128]{3,2,1,0:T(8,128)(2,1)} fusion(bf16[32,128,256]{2,1,0:T(8,128)(2,1)} %gather_fusion.2, pred[32]{0:T(512)(128)(4,1)S(1)} %get-tuple-element.63, bf16[32,128,256]{2,1,0:T(8,128)(2,1)} %gather_fusion, pred[32]{0:T(512)(128)(4,1)S(1)} %get-tuple-element.69), kind=kOutput, calls=%fused_computation.18 | convolution fusion | flops 271581184 | bytes 5242944 | tf_op jit(solution)/shard_map/spif,spjf->spij/dot_general | solution.py:124
  86.2 0.7 copy.40
  (29 shorter events, 0.4 us)
Async XLA Ops:
  0.6 17.6 %copy-start = (bf16[1,32,128,128]{3,2,1,0:T(8,128)(2,1)S(1)}, bf16[1,32,128,128]{3,2,1,0:T(8,128)(2,1)}, u32[]{:S(2)}) copy-start(bf16[1,32,128,128]{3,2,1,0:T(8,128)(2,1)} %param.22) | copy-start | bytes 3145732
  0.6 10.1 %collective-permute-start = (bf16[1,512,256]{2,1,0:T(8,128)(2,1)}, bf16[1,512,256]{2,1,0:T(8,128)(2,1)S(1)}, u32[]{:S(2)}, u32[]{:S(2)}) collective-permute-start(bf16[1,512,256]{2,1,0:T(8,128)(2,1)} %param.18), channel_id=1, source_target_pairs={{0,1},{1,2},{2,3},{3,4},{4,5},{5,6},{6,7},{7,8},{8,9},{9,10},{10,1... | collective-permute-start | bytes 786440 | tf_op jit(solution)/shard_map/ppermute | solution.py:17
  6.1 9.1 %collective-permute-start.1 = (bf16[1,512,256]{2,1,0:T(8,128)(2,1)}, bf16[1,512,256]{2,1,0:T(8,128)(2,1)S(1)}, u32[]{:S(2)}, u32[]{:S(2)}) collective-permute-start(bf16[1,512,256]{2,1,0:T(8,128)(2,1)} %param.18), channel_id=1, source_target_pairs={{1,0},{2,1},{3,2},{4,3},{5,4},{6,5},{7,6},{8,7},{9,8},{10,9},{11,1... | collective-permute-start | bytes 786440 | tf_op jit(solution)/shard_map/ppermute | solution.py:19
  28.1 3.8 %copy-start.1 = (bf16[1,512,256]{2,1,0:T(8,128)(2,1)S(1)}, bf16[1,512,256]{2,1,0:T(8,128)(2,1)}, u32[]{:S(2)}) copy-start(bf16[1,512,256]{2,1,0:T(8,128)(2,1)} %param.18) | copy-start | bytes 786436
  28.1 4.0 %copy-start.4 = (f32[256]{0:T(256)S(1)}, f32[256]{0:T(256)}, u32[]{:S(2)}) copy-start(f32[256]{0:T(256)} %param.23) | copy-start | bytes 3076
  31.9 11.1 %copy-start.5 = (s32[1,32]{1,0:T(1,128)S(1)}, s32[1,32]{1,0:T(1,128)}, u32[]{:S(2)}) copy-start(s32[1,32]{1,0:T(1,128)} %param.31) | copy-start | bytes 388
  31.9 11.1 %copy-start.6 = (s32[1,32]{1,0:T(1,128)S(1)}, s32[1,32]{1,0:T(1,128)}, u32[]{:S(2)}) copy-start(s32[1,32]{1,0:T(1,128)} %param.30) | copy-start | bytes 388
  32.2 18.3 %copy-start.2 = (bf16[256,512]{1,0:T(8,128)(2,1)S(1)}, bf16[256,512]{1,0:T(8,128)(2,1)}, u32[]{:S(2)}) copy-start(bf16[256,512]{1,0:T(8,128)(2,1)} %param.24) | copy-start | bytes 786436
  36.2 14.1 %all-to-all-start = ((bf16[16,2,4096]{2,1,0:T(2,128)(2,1)}), bf16[16,2,4096]{2,1,0:T(2,128)(2,1)S(1)}, u32[]{:S(2)}, u32[]{:S(2)}) async-start(bf16[16,2,4096]{2,1,0:T(2,128)(2,1)} %reshape.205), calls=%async_computation | async-start | bytes 524288 | tf_op jit(solution)/shard_map/all_to_all | solution.py:108
  50.9 1.1 %copy-start.7 = (f32[256]{0:T(256)S(1)}, f32[256]{0:T(256)}, u32[]{:S(2)}) copy-start(f32[256]{0:T(256)} %param.26) | copy-start | bytes 3076
  52.0 21.3 %copy-start.3 = (bf16[256,256]{1,0:T(8,128)(2,1)S(1)}, bf16[256,256]{1,0:T(8,128)(2,1)}, u32[]{:S(2)}) copy-start(bf16[256,256]{1,0:T(8,128)(2,1)} %param.29) | copy-start | bytes 393220
  54.8 10.8 %all-to-all-start.1 = ((bf16[16,32,256]{2,1,0:T(8,128)(2,1)}), bf16[16,32,256]{2,1,0:T(8,128)(2,1)S(1)}, u32[]{:S(2)}, u32[]{:S(2)}) async-start(bf16[16,32,256]{2,1,0:T(8,128)(2,1)} %fusion.16), calls=%async_computation.1 | async-start | bytes 524288 | tf_op jit(solution)/shard_map/all_to_all | solution.py:112
  65.6 9.8 %collective-permute-start.2 = (bf16[1,512,256]{2,1,0:T(8,128)(2,1)S(1)}, bf16[1,512,256]{2,1,0:T(8,128)(2,1)S(1)}, u32[]{:S(2)}, u32[]{:S(2)}) collective-permute-start(bf16[1,512,256]{2,1,0:T(8,128)(2,1)S(1)} %bitcast.108), channel_id=1, source_target_pairs={{0,1},{1,2},{2,3},{3,4},{4,5},{5,6},{6,7},{7,8},{8,9},{9,10},{10,1... | collective-permute-start | bytes 786440 | tf_op jit(solution)/shard_map/ppermute | solution.py:17
  71.3 8.9 %collective-permute-start.3 = (bf16[1,512,256]{2,1,0:T(8,128)(2,1)S(1)}, bf16[1,512,256]{2,1,0:T(8,128)(2,1)S(1)}, u32[]{:S(2)}, u32[]{:S(2)}) collective-permute-start(bf16[1,512,256]{2,1,0:T(8,128)(2,1)S(1)} %bitcast.109), channel_id=1, source_target_pairs={{1,0},{2,1},{3,2},{4,3},{5,4},{6,5},{7,6},{8,7},{9,8},{10,9},{11,1... | collective-permute-start | bytes 786440 | tf_op jit(solution)/shard_map/ppermute | solution.py:19
where the time goes:
time: 87.6 us; the launch traced here: 86.9 us
  starting transfers between devices  25.2 us (29%)
  waiting for transfers between devices  23.7 us (27%)
  matrix products  15.4 us (18%)
  local copies, waits for them, and re-layouts  14.4 us (16%)
  other arithmetic  6.3 us (7%)
  between operations  1.6 us (2%)
    ppermute x2, starting transfers between devices, with_halo(): lax.ppermute(tail, axis, [(i, (i + 1) % count) for i in range(ends)])  11.1 us
    ppermute x2, waiting for transfers between devices, with_halo(): lax.ppermute(head, axis, [((i + 1) % count, i) for i in range(ends)])  9.16 us
    all_to_all x1, waiting for transfers between devices, body(): lax.all_to_all(vertex_out, 'snap', split_axis=0, concat_axis=1, tiled=True)  7.28 us
    all_to_all x1, waiting for transfers between devices, body(): lax.all_to_all(normed, 'snap', split_axis=1, concat_axis=0, tiled=True)  7.26 us
    all_to_all x1, starting transfers between devices, body(): lax.all_to_all(normed, 'snap', split_axis=1, concat_axis=0, tiled=True)  6.75 us
    gather x6, local copies, waits for them, and re-layouts, pick_blocks(): jnp.take(source_table, chosen, axis=0)  6.03 us
    dot_general x1, local copies, waits for them, and re-layouts, tile_terms(): jnp.einsum('sgij,sgjf->sgif', tile_part, picked, preferred_element_type=j...  5.47 us
    dot_general x1, matrix products, tile_terms(): jnp.einsum('sgij,sgjf->sgif', tile_part, picked, preferred_element_type=j...  4.37 us
  transfers between devices with their start and end apart: 6, of which 4 were waited for; matrix products, arithmetic and copies ran while one was open for 5% of the time, Pallas kernels for 0%

commit v1 on v0

--- a/solution.py
+++ b/solution.py
@@ -4,6 +4,12 @@
 from jax.sharding import PartitionSpec as P
 
 epsilon = 1e-06
+
+
+def stacked_exchange(block, mesh_axis, split, join):
+    cells = jnp.split(block, lax.axis_size(mesh_axis), axis=split)
+    received = lax.all_to_all(jnp.stack(cells), mesh_axis, 0, 0)
+    return jnp.concatenate(received, axis=join)
 
 
 def with_halo(cells, sides, width):
@@ -105,7 +111,7 @@
         jnp.float32
     )
     normed = root_norm(combined, norm_gain).astype(jnp.bfloat16)
-    by_vertex = lax.all_to_all(normed, "snap", split_axis=1, concat_axis=0, tiled=True)
+    by_vertex = stacked_exchange(normed, "snap", 1, 0)
     decays, drives = gate_drive(by_vertex, decay_rate, mix_weight)
     states = run_states(decays, drives, jnp.zeros(decays.shape[1:], jnp.float32))
     vertex_out = feed_forward(states, mlp_gain, up_weight, down_weight)

time: 87.6 us -> 93.1 us (1.063)
  local copies, waits for them, and re-layouts: 14.4 us -> 22.1 us
  other arithmetic: 6.3 us -> 4.09 us
    unnamed x21 -> x32, local copies, waits for them, and re-layouts: 2.34 us -> 9.85 us
    unnamed x2 -> x1, other arithmetic: 2.21 us -> 0.01 us
where the time goes in v1:
time: 93.1 us; the launch traced here: 92.4 us
  starting transfers between devices  25.2 us (27%)
  waiting for transfers between devices  23.7 us (25%)
  local copies, waits for them, and re-layouts  22.1 us (24%)
  matrix products  15.4 us (17%)
  other arithmetic  4.09 us (4%)
  between operations  1.56 us (2%)
    ppermute x2, starting transfers between devices, with_halo(): lax.ppermute(tail, axis, [(i, (i + 1) % count) for i in range(ends)])  11.1 us
    unnamed x32, local copies, waits for them, and re-layouts  9.85 us
    ppermute x2, waiting for transfers between devices, with_halo(): lax.ppermute(head, axis, [((i + 1) % count, i) for i in range(ends)])  9.16 us
    all_to_all x1, waiting for transfers between devices, body(): lax.all_to_all(vertex_out, 'snap', split_axis=0, concat_axis=1, tiled=True)  7.28 us
    all_to_all x1, waiting for transfers between devices, stacked_exchange(): received = lax.all_to_all(jnp.stack(cells), mesh_axis, 0, 0)  7.26 us
    all_to_all x1, starting transfers between devices, stacked_exchange(): received = lax.all_to_all(jnp.stack(cells), mesh_axis, 0, 0)  6.75 us
    gather x6, local copies, waits for them, and re-layouts, pick_blocks(): jnp.take(source_table, chosen, axis=0)  6.06 us
    dot_general x1, local copies, waits for them, and re-layouts, tile_terms(): jnp.einsum('sgij,sgjf->sgif', tile_part, picked, preferred_element_type=j...  5.48 us
  transfers between devices with their start and end apart: 6, of which 4 were waited for; matrix products, arithmetic and copies ran while one was open for 5% of the time, Pallas kernels for 0%

profile of v1, /device:TPU:97, one launch (start us, length us, event | category | flops | bytes accessed | tf_op | source)
XLA Modules:
  0.0 92.4 jit_solution(9433325267545814258)
XLA Ops:
  0.6 0.0 copy-start
  0.6 5.5 %collective-permute-start = (bf16[1,512,256]{2,1,0:T(8,128)(2,1)}, bf16[1,512,256]{2,1,0:T(8,128)(2,1)S(1)}, u32[]{:S(2)}, u32[]{:S(2)}) collective-permute-start(bf16[1,512,256]{2,1,0:T(8,128)(2,1)} %param.18), channel_id=1, source_target_pairs={{0,1},{1,2},{2,3},{3,4},{4,5},{5,6},{6,7},{7,8},{8,9},{9,10},{10,1... | collective-permute-start | bytes 786440 | tf_op jit(solution)/shard_map/ppermute | solution.py:23
  6.1 1.9 %collective-permute-start.1 = (bf16[1,512,256]{2,1,0:T(8,128)(2,1)}, bf16[1,512,256]{2,1,0:T(8,128)(2,1)S(1)}, u32[]{:S(2)}, u32[]{:S(2)}) collective-permute-start(bf16[1,512,256]{2,1,0:T(8,128)(2,1)} %param.18), channel_id=1, source_target_pairs={{1,0},{2,1},{3,2},{4,3},{5,4},{6,5},{7,6},{8,7},{9,8},{10,9},{11,1... | collective-permute-start | bytes 786440 | tf_op jit(solution)/shard_map/ppermute | solution.py:25
  8.0 0.7 and_bitcast_fusion.1
  9.4 0.7 subtract_bitcast_fusion
  10.0 0.7 neg.11
  10.8 0.0 collective-permute-done
  10.8 4.4 %collective-permute-done.1 = bf16[1,512,256]{2,1,0:T(8,128)(2,1)S(1)} collective-permute-done((bf16[1,512,256]{2,1,0:T(8,128)(2,1)}, bf16[1,512,256]{2,1,0:T(8,128)(2,1)S(1)}, u32[]{:S(2)}, u32[]{:S(2)}) %collective-permute-start.1) | collective-permute-done | bytes 262176 | tf_op jit(solution)/shard_map/ppermute | solution.py:25
  15.2 1.0 %pad_maximum_fusion = bf16[1,1536,256]{2,1,0:T(8,128)(2,1)S(1)} fusion(bf16[1,512,256]{2,1,0:T(8,128)(2,1)S(1)} %collective-permute-done.1, bf16[1,512,256]{2,1,0:T(8,128)(2,1)} %param.18, bf16[1,512,256]{2,1,0:T(8,128)(2,1)S(1)} %collective-permute-done), kind=kLoop, calls=%fused_computation.27 | loop fusion | flops 2359296 | bytes 1572864 | tf_op jit(solution)/shard_map/concatenate | solution.py:21
  16.2 2.0 %gather_fusion.1 = bf16[32,128,256]{2,1,0:T(8,128)(2,1)} fusion(bf16[1,12,128,256]{3,2,1,0:T(8,128)(2,1)S(1)} %bitcast.165, s32[32]{0:T(128)S(1)} %or_bitcast_fusion.1), kind=kCustom, calls=%fused_computation.clone | custom fusion | bytes 4194560 | tf_op jit(solution)/shard_map/vmap(jit(_take))/gather | solution.py:41
  18.2 0.0 copy-done
  18.2 4.4 %convolution_bitcast_fusion = f32[32,128,256]{1,2,0:T(8,128)} fusion(bf16[32,128,256]{2,1,0:T(8,128)(2,1)} %gather_fusion.1, pred[32]{0:T(512)(128)(4,1)S(1)} %get-tuple-element.67, bf16[1,32,128,128]{3,2,1,0:T(8,128)(2,1)S(1)} %copy-done), kind=kOutput, calls=%fused_computation.6 | convolution fusion | flops 269484032 | bytes 7340064 | tf_op jit(solution)/shard_map/sgij,sgjf->sgif/dot_general | solution.py:48
  22.6 5.5 %copy.50 = f32[32,128,256]{2,0,1:T(8,128)} copy(f32[32,128,256]{1,2,0:T(8,128)} %convolution_bitcast_fusion) | data formatting | bytes 8388608 | tf_op jit(solution)/shard_map/sgij,sgjf->sgif/dot_general | solution.py:48
  28.1 3.7 %fusion.39 = f32[4,128,256]{2,0,1:T(4,128)S(1)} fusion(f32[32,128,256]{2,0,1:T(8,128)} %copy.50, s32[32]{0:T(128)S(1)} %subtract_bitcast_fusion, pred[32]{0:T(512)(128)(4,1)S(1)} %iota_compare_fusion.1), kind=kOutput, calls=%fused_computation.88 | convolution fusion | flops 50331904 | bytes 4718752 | tf_op jit(solution)/shard_map/sgb,sgif->sbif/dot_general | solution.py:51
  31.8 0.0 copy-start.5
  31.8 0.0 copy-start.6
  31.8 0.0 copy-start.2
  31.8 0.1 copy.51
  31.9 0.0 copy-done.1
  32.0 0.2 multiply_reduce_fusion.1
  32.1 0.0 copy-done.4
  32.1 0.1 multiply_convert_fusion.5
  32.3 0.6 constant_dynamic-update-slice_fusion.15
  32.9 0.6 constant_dynamic-update-slice_fusion.14
  33.5 0.6 constant_dynamic-update-slice_fusion.13
  34.1 0.6 constant_dynamic-update-slice_fusion.12
  34.7 0.6 constant_dynamic-update-slice_fusion.11
  35.3 0.6 constant_dynamic-update-slice_fusion.10
  35.9 0.6 constant_dynamic-update-slice_fusion.9
  36.5 0.6 constant_dynamic-update-slice_fusion.8
  37.1 0.6 constant_dynamic-update-slice_fusion.7
  37.8 0.6 constant_dynamic-update-slice_fusion.6
  38.4 0.6 constant_dynamic-update-slice_fusion.5
  39.0 0.6 constant_dynamic-update-slice_fusion.4
  39.6 0.6 constant_dynamic-update-slice_fusion.3
  40.2 0.6 constant_dynamic-update-slice_fusion.2
  40.8 0.6 constant_dynamic-update-slice_fusion.1
  41.4 0.6 constant_dynamic-update-slice_fusion
  42.0 6.8 %all-to-all-start = ((bf16[16,1,32,256]{3,2,1,0:T(8,128)(2,1)}), bf16[16,1,32,256]{3,2,1,0:T(8,128)(2,1)S(1)}, u32[]{:S(2)}, u32[]{:S(2)}) async-start(bf16[16,1,32,256]{3,2,1,0:T(8,128)(2,1)} %constant_dynamic-update-slice_fusion), calls=%async_computation | async-start | bytes 524288 | tf_op jit(solution)/shard_map/all_to_all | solution.py:11
  48.8 0.0 copy-done.5
  48.8 0.0 copy-done.6
  48.8 7.3 %all-to-all-done = bf16[16,1,32,256]{3,2,1,0:T(8,128)(2,1)S(1)} async-done(((bf16[16,1,32,256]{3,2,1,0:T(8,128)(2,1)}), bf16[16,1,32,256]{3,2,1,0:T(8,128)(2,1)S(1)}, u32[]{:S(2)}, u32[]{:S(2)}) %all-to-all-start) | async-done | bytes 262176 | tf_op jit(solution)/shard_map/all_to_all | solution.py:11
  56.1 0.0 copy-done.2
  56.1 0.3 fusion.30
  56.4 0.0 copy-start.7
  56.4 0.2 slice_multiply_fusion
  56.6 0.6 while.13
  57.3 0.1 multiply_reduce_fusion
  57.4 0.0 copy-done.7
  57.5 0.0 copy-start.3
  57.5 2.8 %fusion.16 = bf16[16,32,256]{2,1,0:T(8,128)(2,1)} fusion(f32[16,32,256]{2,1,0:T(8,128)S(1)} %get-tuple-element.30, bf16[1024,256]{1,0:T(8,128)(2,1)} %param.28, bf16[256,1024]{1,0:T(8,128)(2,1)} %param.27, f32[256]{0:T(256)S(1)} %copy-done.7, f32[16,32]{1,0:T(8,128)S(1)} %add_rsqrt_fusion), kind=kOutput, calls=%fused_computation.20 | convolution fusion | flops 540147712 | bytes 1838080 | tf_op jit(solution)/shard_map/tnh,hf->tnf/dot_general | solution.py:77
  60.3 3.5 %all-to-all-start.1 = ((bf16[16,32,256]{2,1,0:T(8,128)(2,1)}), bf16[16,32,256]{2,1,0:T(8,128)(2,1)S(1)}, u32[]{:S(2)}, u32[]{:S(2)}) async-start(bf16[16,32,256]{2,1,0:T(8,128)(2,1)} %fusion.16), calls=%async_computation.1 | async-start | bytes 524288 | tf_op jit(solution)/shard_map/all_to_all | solution.py:118
  63.8 7.3 %all-to-all-done.1 = bf16[16,32,256]{2,1,0:T(8,128)(2,1)S(1)} async-done(((bf16[16,32,256]{2,1,0:T(8,128)(2,1)}), bf16[16,32,256]{2,1,0:T(8,128)(2,1)S(1)}, u32[]{:S(2)}, u32[]{:S(2)}) %all-to-all-start.1) | async-done | bytes 262176 | tf_op jit(solution)/shard_map/all_to_all | solution.py:118
  71.1 5.6 %collective-permute-start.2 = (bf16[1,512,256]{2,1,0:T(8,128)(2,1)S(1)}, bf16[1,512,256]{2,1,0:T(8,128)(2,1)S(1)}, u32[]{:S(2)}, u32[]{:S(2)}) collective-permute-start(bf16[1,512,256]{2,1,0:T(8,128)(2,1)S(1)} %bitcast.169), channel_id=1, source_target_pairs={{0,1},{1,2},{2,3},{3,4},{4,5},{5,6},{6,7},{7,8},{8,9},{9,10},{10,1... | collective-permute-start | bytes 786440 | tf_op jit(solution)/shard_map/ppermute | solution.py:23
  76.8 1.9 %collective-permute-start.3 = (bf16[1,512,256]{2,1,0:T(8,128)(2,1)S(1)}, bf16[1,512,256]{2,1,0:T(8,128)(2,1)S(1)}, u32[]{:S(2)}, u32[]{:S(2)}) collective-permute-start(bf16[1,512,256]{2,1,0:T(8,128)(2,1)S(1)} %bitcast.170), channel_id=1, source_target_pairs={{1,0},{2,1},{3,2},{4,3},{5,4},{6,5},{7,6},{8,7},{9,8},{10,9},{11,1... | collective-permute-start | bytes 786440 | tf_op jit(solution)/shard_map/ppermute | solution.py:25
  78.7 0.0 copy-done.3
  78.7 0.2 convolution_convert_fusion
  79.0 2.0 %gather_fusion = bf16[32,128,256]{2,1,0:T(8,128)(2,1)} fusion(bf16[1,4,128,256]{3,2,1,0:T(8,128)(2,1)S(1)} %bitcast.164, s32[32]{0:T(128)S(1)} %or_bitcast_fusion.2), kind=kCustom, calls=%fused_computation.2 | custom fusion | bytes 4194560 | tf_op jit(solution)/shard_map/vmap(jit(_take))/gather | solution.py:41
  81.0 0.0 collective-permute-done.2
  81.0 4.7 %collective-permute-done.3 = bf16[1,512,256]{2,1,0:T(8,128)(2,1)S(1)} collective-permute-done((bf16[1,512,256]{2,1,0:T(8,128)(2,1)S(1)}, bf16[1,512,256]{2,1,0:T(8,128)(2,1)S(1)}, u32[]{:S(2)}, u32[]{:S(2)}) %collective-permute-start.3) | collective-permute-done | bytes 262176 | tf_op jit(solution)/shard_map/ppermute | solution.py:25
  85.7 0.1 pad_maximum_fusion.1
  85.7 2.0 %gather_fusion.2 = bf16[32,128,256]{2,1,0:T(8,128)(2,1)} fusion(bf16[1,12,128,256]{3,2,1,0:T(8,128)(2,1)S(1)} %bitcast.166, s32[32]{0:T(128)S(1)} %or_bitcast_fusion), kind=kCustom, calls=%fused_computation.1.clone | custom fusion | bytes 4194560 | tf_op jit(solution)/shard_map/vmap(jit(_take))/gather | solution.py:41
  87.7 4.0 %fusion.11 = bf16[1,32,128,128]{3,2,1,0:T(8,128)(2,1)} fusion(bf16[32,128,256]{2,1,0:T(8,128)(2,1)} %gather_fusion.2, pred[32]{0:T(512)(128)(4,1)S(1)} %get-tuple-element.63, bf16[32,128,256]{2,1,0:T(8,128)(2,1)} %gather_fusion, pred[32]{0:T(512)(128)(4,1)S(1)} %get-tuple-element.69), kind=kOutput, calls=%fused_computation.18 | convolution fusion | flops 271581184 | bytes 5242944 | tf_op jit(solution)/shard_map/spif,spjf->spij/dot_general | solution.py:130
  91.7 0.7 copy.80
  (30 shorter events, 0.3 us)
Async XLA Ops:
  0.6 17.6 %copy-start = (bf16[1,32,128,128]{3,2,1,0:T(8,128)(2,1)S(1)}, bf16[1,32,128,128]{3,2,1,0:T(8,128)(2,1)}, u32[]{:S(2)}) copy-start(bf16[1,32,128,128]{3,2,1,0:T(8,128)(2,1)} %param.22) | copy-start | bytes 3145732
  0.6 10.1 %collective-permute-start = (bf16[1,512,256]{2,1,0:T(8,128)(2,1)}, bf16[1,512,256]{2,1,0:T(8,128)(2,1)S(1)}, u32[]{:S(2)}, u32[]{:S(2)}) collective-permute-start(bf16[1,512,256]{2,1,0:T(8,128)(2,1)} %param.18), channel_id=1, source_target_pairs={{0,1},{1,2},{2,3},{3,4},{4,5},{5,6},{6,7},{7,8},{8,9},{9,10},{10,1... | collective-permute-start | bytes 786440 | tf_op jit(solution)/shard_map/ppermute | solution.py:23
  6.1 9.1 %collective-permute-start.1 = (bf16[1,512,256]{2,1,0:T(8,128)(2,1)}, bf16[1,512,256]{2,1,0:T(8,128)(2,1)S(1)}, u32[]{:S(2)}, u32[]{:S(2)}) collective-permute-start(bf16[1,512,256]{2,1,0:T(8,128)(2,1)} %param.18), channel_id=1, source_target_pairs={{1,0},{2,1},{3,2},{4,3},{5,4},{6,5},{7,6},{8,7},{9,8},{10,9},{11,1... | collective-permute-start | bytes 786440 | tf_op jit(solution)/shard_map/ppermute | solution.py:25
  28.1 3.8 %copy-start.1 = (bf16[1,512,256]{2,1,0:T(8,128)(2,1)S(1)}, bf16[1,512,256]{2,1,0:T(8,128)(2,1)}, u32[]{:S(2)}) copy-start(bf16[1,512,256]{2,1,0:T(8,128)(2,1)} %param.18) | copy-start | bytes 786436
  28.1 4.0 %copy-start.4 = (f32[256]{0:T(256)S(1)}, f32[256]{0:T(256)}, u32[]{:S(2)}) copy-start(f32[256]{0:T(256)} %param.23) | copy-start | bytes 3076
  31.8 17.0 %copy-start.5 = (s32[1,32]{1,0:T(1,128)S(1)}, s32[1,32]{1,0:T(1,128)}, u32[]{:S(2)}) copy-start(s32[1,32]{1,0:T(1,128)} %param.31) | copy-start | bytes 388
  31.8 17.0 %copy-start.6 = (s32[1,32]{1,0:T(1,128)S(1)}, s32[1,32]{1,0:T(1,128)}, u32[]{:S(2)}) copy-start(s32[1,32]{1,0:T(1,128)} %param.30) | copy-start | bytes 388
  31.8 24.3 %copy-start.2 = (bf16[256,512]{1,0:T(8,128)(2,1)S(1)}, bf16[256,512]{1,0:T(8,128)(2,1)}, u32[]{:S(2)}) copy-start(bf16[256,512]{1,0:T(8,128)(2,1)} %param.24) | copy-start | bytes 786436
  42.0 14.1 %all-to-all-start = ((bf16[16,1,32,256]{3,2,1,0:T(8,128)(2,1)}), bf16[16,1,32,256]{3,2,1,0:T(8,128)(2,1)S(1)}, u32[]{:S(2)}, u32[]{:S(2)}) async-start(bf16[16,1,32,256]{3,2,1,0:T(8,128)(2,1)} %constant_dynamic-update-slice_fusion), calls=%async_computation | async-start | bytes 524288 | tf_op jit(solution)/shard_map/all_to_all | solution.py:11
  56.4 1.1 %copy-start.7 = (f32[256]{0:T(256)S(1)}, f32[256]{0:T(256)}, u32[]{:S(2)}) copy-start(f32[256]{0:T(256)} %param.26) | copy-start | bytes 3076
  57.5 21.3 %copy-start.3 = (bf16[256,256]{1,0:T(8,128)(2,1)S(1)}, bf16[256,256]{1,0:T(8,128)(2,1)}, u32[]{:S(2)}) copy-start(bf16[256,256]{1,0:T(8,128)(2,1)} %param.29) | copy-start | bytes 393220
  60.3 10.8 %all-to-all-start.1 = ((bf16[16,32,256]{2,1,0:T(8,128)(2,1)}), bf16[16,32,256]{2,1,0:T(8,128)(2,1)S(1)}, u32[]{:S(2)}, u32[]{:S(2)}) async-start(bf16[16,32,256]{2,1,0:T(8,128)(2,1)} %fusion.16), calls=%async_computation.1 | async-start | bytes 524288 | tf_op jit(solution)/shard_map/all_to_all | solution.py:118
  71.1 9.8 %collective-permute-start.2 = (bf16[1,512,256]{2,1,0:T(8,128)(2,1)S(1)}, bf16[1,512,256]{2,1,0:T(8,128)(2,1)S(1)}, u32[]{:S(2)}, u32[]{:S(2)}) collective-permute-start(bf16[1,512,256]{2,1,0:T(8,128)(2,1)S(1)} %bitcast.169), channel_id=1, source_target_pairs={{0,1},{1,2},{2,3},{3,4},{4,5},{5,6},{6,7},{7,8},{8,9},{9,10},{10,1... | collective-permute-start | bytes 786440 | tf_op jit(solution)/shard_map/ppermute | solution.py:23
  76.8 8.9 %collective-permute-start.3 = (bf16[1,512,256]{2,1,0:T(8,128)(2,1)S(1)}, bf16[1,512,256]{2,1,0:T(8,128)(2,1)S(1)}, u32[]{:S(2)}, u32[]{:S(2)}) collective-permute-start(bf16[1,512,256]{2,1,0:T(8,128)(2,1)S(1)} %bitcast.170), channel_id=1, source_target_pairs={{1,0},{2,1},{3,2},{4,3},{5,4},{6,5},{7,6},{8,7},{9,8},{10,9},{11,1... | collective-permute-start | bytes 786440 | tf_op jit(solution)/shard_map/ppermute | solution.py:25
